TPU v7x, 32 devices: a whole 2x2x4 slice. The times are simulated.
32 devices in a mesh: seq: 16 (over z, y, x), head: 2 (over core).
Axes of the slice: x: 2, y: 2, z: 4, core: 2. Of those that a mesh axis runs over, the one named last changes fastest.
Arguments:
- tokens: bfloat16 [2048, 2048], P('seq'), may hold values from -6 to 6
- norm1_gain: float32 [2048], replicated, may hold values from 0.1 to 1.9
- mix_weight: bfloat16 [4, 2048, 2048], P(None, 'seq', 'head'), may hold values from -0.125 to 0.125
- conv_weight: float32 [3, 4, 2048], P(None, None, 'head'), may hold values from -3 to 3
- decay_gap: float32 [2048], P('head'), may hold values from 0.00024414062 to 0.05
- group_gain: float32 [2048], P('head'), may hold values from 0.1 to 1.9
- out_weight: bfloat16 [2048, 2048], P('head', 'seq'), may hold values from -0.25 to 0.25
- norm2_gain: float32 [2048], replicated, may hold values from 0.1 to 1.9
- up_pair: bfloat16 [2, 2048, 5632], P(None, 'seq', 'head'), may hold values from -0.125 to 0.125
- down_weight: bfloat16 [5632, 2048], P('head', 'seq'), may hold values from -0.078125 to 0.078125
- cotangent: bfloat16 [2048, 2048], P('seq'), may hold values from -6 to 6
Outputs:
- block_out: float32 [2048, 2048], P('seq')
- grad_tokens: float32 [2048, 2048], P('seq')
- grad_norm1: float32 [2048], replicated
- grad_mix: float32 [4, 2048, 2048], P(None, 'seq', 'head')
- grad_conv: float32 [3, 4, 2048], P(None, None, 'head')
- grad_gap: float32 [2048], P('head')
- grad_group: float32 [2048], P('head')
- grad_out: float32 [2048, 2048], P('head', 'seq')
- grad_norm2: float32 [2048], replicated
- grad_up: float32 [2, 2048, 5632], P(None, 'seq', 'head')
- grad_down: float32 [5632, 2048], P('head', 'seq')
- inverse_rms: float32 [2, 2048], P(None, 'seq')
All inputs are finite; a program needn't handle non-finite values.
Results may differ from a plain program's by a relative error of at most 0.012.
Values may be sent and summed in bfloat16 or wider, within the bound.
No kernel may reach another device: no remote copies, remote signals or barrier semaphores. Data moves between devices by JAX's collectives and lax.ppermute only.
A program may use at most 320 MiB of HBM per device.

v0:
```python
import jax
import jax.numpy as jnp
from jax import lax
from jax.sharding import PartitionSpec as P

HEAD_DIM = 128
SPAN = 64
EPS_TOKEN = 1e-06
EPS_GROUP = 1e-05
HIGH = lax.Precision.HIGHEST


def from_behind(value, axis, steps):
    count = lax.axis_size(axis)
    first, last = (max(0, -steps), min(count, count - steps))
    return lax.ppermute(value, axis, [(source, source + steps) for source in range(first, last)])


def carried_in(array, axis, combine, identity, reverse):
    peers, here = (lax.axis_size(axis), lax.axis_index(axis))
    everything = jax.tree.map(lambda part: lax.all_gather(part, axis), array)
    start = jax.tree.map(
        lambda part, zero: jnp.broadcast_to(jnp.asarray(zero, part.dtype), part.shape),
        array,
        identity,
    )

    def turn(k, before):
        at = peers - 1 - k if reverse else k
        reached = at > here if reverse else at < here
        new = combine(before, jax.tree.map(lambda part: part[at], everything))
        return jax.tree.map(lambda a, b: jnp.where(reached, a, b), new, before)

    return lax.fori_loop(0, peers, turn, start)


def silu_grad(inputs_val):
    sigmoid_val = jax.nn.sigmoid(inputs_val)
    return sigmoid_val * (1.0 + inputs_val * (1.0 - sigmoid_val))


def token_norm(token_rows, gain_vec):
    inverse = lax.rsqrt(jnp.mean(token_rows * token_rows, axis=-1, keepdims=True) + EPS_TOKEN)
    return (token_rows * inverse * gain_vec, inverse)


def token_norm_back(token_rows, inverse, gain_vec, grad_in):
    scaled = grad_in * gain_vec
    dot_term = jnp.mean(scaled * token_rows, axis=-1, keepdims=True)
    grad_rows = inverse * scaled - token_rows * inverse * inverse * inverse * dot_term
    grad_gain = jnp.sum(grad_in * token_rows * inverse, axis=0)
    return (grad_rows, grad_gain)


def convolve(extended, conv_taps):
    length = extended.shape[1] - 3
    total = conv_taps[:, 0][:, None] * extended[:, 3:]
    for delay_step in range(1, 4):
        total = (
            total
            + conv_taps[:, delay_step][:, None]
            * extended[:, 3 - delay_step : 3 - delay_step + length]
        )
    return total


def gates(convolved, decay_gap):
    queries = jax.nn.silu(convolved[0])
    open_share = 1.0 - jax.nn.sigmoid(convolved[1])
    log_forget = jnp.log(1.0 - decay_gap * open_share)
    key_rows = decay_gap * open_share
    return (queries, log_forget, key_rows, convolved[2])


def span_step(carry_state, pieces):
    queries, log_forget, key_rows, values = pieces
    running = jnp.cumsum(log_forget, axis=0)
    decayed_query = queries * jnp.exp(running)
    lifted_key = key_rows * jnp.exp(-running)
    scores = jnp.einsum("thd,shd->hts", decayed_query, lifted_key, precision=HIGH)
    causal = jnp.arange(SPAN)[:, None] >= jnp.arange(SPAN)[None, :]
    scores = jnp.where(causal[None], scores, 0.0)
    mixed_out = jnp.einsum("hts,she->the", scores, values, precision=HIGH)
    mixed_out = mixed_out + jnp.einsum("thd,hde->the", decayed_query, carry_state, precision=HIGH)
    final_log = running[-1]
    carried = key_rows * jnp.exp(final_log[None] - running)
    carry_state = jnp.exp(final_log)[:, :, None] * carry_state + jnp.einsum(
        "thd,the->hde", carried, values, precision=HIGH
    )
    return (carry_state, mixed_out)


def local_mix(queries, log_forget, key_rows, values, state_in):
    length, heads_here, head_width = queries.shape
    blocks = length // SPAN

    def blocked(array):
        return array.reshape(blocks, SPAN, heads_here, head_width)

    state_out, mixed_out = lax.scan(
        jax.checkpoint(span_step),
        state_in,
        (blocked(queries), blocked(log_forget), blocked(key_rows), blocked(values)),
    )
    return (mixed_out.reshape(length, heads_here, head_width), state_out)


def running_log(log_forget):
    length = log_forget.shape[0]
    blocked = log_forget.reshape((length // SPAN, SPAN) + log_forget.shape[1:])
    inside = jnp.cumsum(blocked, axis=1)
    totals = inside[:, -1]
    before = jnp.cumsum(totals, axis=0) - totals
    return (inside + before[:, None]).reshape(log_forget.shape)


def group_gate(mixed_out, gate_rows, group_gain):
    inverse = lax.rsqrt(jnp.mean(mixed_out * mixed_out, axis=-1, keepdims=True) + EPS_GROUP)
    normed = (mixed_out * inverse).reshape(gate_rows.shape)
    return normed * group_gain * jax.nn.silu(gate_rows)


def split_heads(array):
    return array.reshape(array.shape[0], -1, HEAD_DIM)


def merge_heads(array):
    return array.reshape(array.shape[0], -1)


def combine_state(earlier, later):
    return (earlier[0] * later[0], later[0][..., None] * earlier[1] + later[1])


def head_total(partial_sum):
    share = lax.psum_scatter(partial_sum, "head", scatter_dimension=1, tiled=True)
    return lax.all_gather(share, "head", axis=1, tiled=True)


def shards(
    tokens,
    norm1_gain,
    mix_weight,
    conv_weight,
    decay_gap,
    group_gain,
    out_weight,
    norm2_gain,
    up_pair,
    down_weight,
    cotangent,
):
    mix_full, up_full, out_full, down_full = (
        lax.all_gather(mix_weight, "seq", axis=1, tiled=True),
        lax.all_gather(up_pair, "seq", axis=1, tiled=True),
        lax.all_gather(out_weight, "seq", axis=1, tiled=True),
        lax.all_gather(down_weight, "seq", axis=1, tiled=True),
    )
    token_rows = tokens.astype(jnp.float32)
    normed1, inverse1 = token_norm(token_rows, norm1_gain)
    normed1_low = normed1.astype(jnp.bfloat16)
    projected = jnp.einsum(
        "td,jdc->jtc", normed1_low, mix_full, preferred_element_type=jnp.float32
    ).astype(jnp.bfloat16)
    length = projected.shape[1]
    earlier_rows = from_behind(projected[:3, length - 3 :], "seq", 1)
    extended = jnp.concatenate([earlier_rows, projected[:3]], axis=1).astype(jnp.float32)
    convolved, conv_back = jax.vjp(convolve, extended, conv_weight)
    (queries, log_forget, key_rows, values), gate_back = jax.vjp(gates, convolved, decay_gap)
    query_heads = split_heads(queries)
    forget_heads = split_heads(log_forget)
    key_heads = split_heads(key_rows)
    value_heads = split_heads(values)
    log_total = running_log(forget_heads)
    last_log = log_total[-1]
    decay_dev = jnp.exp(last_log)
    own_state = jnp.einsum(
        "thd,the->hde", key_heads * jnp.exp(last_log[None] - log_total), value_heads, precision=HIGH
    )
    identity = (jnp.ones_like(decay_dev), jnp.zeros_like(own_state))
    prior_decay, state_in = carried_in(
        (decay_dev, own_state), "seq", combine_state, identity, False
    )
    (mixed_out, state_end), mix_back = jax.vjp(
        local_mix, query_heads, forget_heads, key_heads, value_heads, state_in
    )
    gate_rows = projected[3].astype(jnp.float32)
    gated, group_back = jax.vjp(group_gate, mixed_out, gate_rows, group_gain)
    gated_low = gated.astype(jnp.bfloat16)
    hidden = token_rows + head_total(
        jnp.dot(gated_low, out_full, preferred_element_type=jnp.float32)
    )
    normed2, inverse2 = token_norm(hidden, norm2_gain)
    normed2_low = normed2.astype(jnp.bfloat16)
    lifted = jnp.einsum("td,jdf->jtf", normed2_low, up_full, preferred_element_type=jnp.float32)
    gate_act = jax.nn.silu(lifted[0])
    inner_act = (gate_act * lifted[1]).astype(jnp.bfloat16)
    block_out = hidden + head_total(
        jnp.dot(inner_act, down_full, preferred_element_type=jnp.float32)
    )
    mix_again, up_again, out_again, down_again = (
        lax.all_gather(mix_weight, "seq", axis=1, tiled=True),
        lax.all_gather(up_pair, "seq", axis=1, tiled=True),
        lax.all_gather(out_weight, "seq", axis=1, tiled=True),
        lax.all_gather(down_weight, "seq", axis=1, tiled=True),
    )
    upstream = cotangent.astype(jnp.float32)
    grad_down = jnp.einsum("tf,td->fd", inner_act, cotangent, preferred_element_type=jnp.float32)
    grad_inner = jnp.einsum("td,fd->tf", cotangent, down_again, preferred_element_type=jnp.float32)
    grad_lifted = jnp.stack(
        [grad_inner * lifted[1] * silu_grad(lifted[0]), grad_inner * gate_act]
    ).astype(jnp.bfloat16)
    grad_up = jnp.einsum(
        "td,jtf->jdf", normed2_low, grad_lifted, preferred_element_type=jnp.float32
    )
    grad_normed2 = head_total(
        jnp.einsum("jtf,jdf->td", grad_lifted, up_again, preferred_element_type=jnp.float32)
    )
    grad_hidden_norm, grad_norm2 = token_norm_back(hidden, inverse2, norm2_gain, grad_normed2)
    grad_hidden = upstream + grad_hidden_norm
    grad_branch = grad_hidden.astype(jnp.bfloat16)
    grad_out = jnp.einsum("tc,td->cd", gated_low, grad_branch, preferred_element_type=jnp.float32)
    grad_gated = jnp.einsum("td,cd->tc", grad_branch, out_again, preferred_element_type=jnp.float32)
    grad_mixed, grad_gate_rows, grad_group = group_back(grad_gated)
    own_grad = jnp.einsum(
        "thd,the->hde", query_heads * jnp.exp(log_total), grad_mixed, precision=HIGH
    )
    later_decay, state_after = carried_in(
        (decay_dev, own_grad), "seq", combine_state, identity, True
    )
    grad_q, grad_f, grad_k, grad_v, grad_start = mix_back((grad_mixed, state_after))
    grad_convolved, grad_gap = gate_back(
        (merge_heads(grad_q), merge_heads(grad_f), merge_heads(grad_k), merge_heads(grad_v))
    )
    grad_extended, grad_conv = conv_back(grad_convolved)
    later_edge = from_behind(grad_extended[:, :3].astype(jnp.bfloat16), "seq", -1).astype(
        jnp.float32
    )
    edge_pad = jnp.concatenate(
        [jnp.zeros((3, length - 3, later_edge.shape[2]), jnp.float32), later_edge], axis=1
    )
    grad_conv_rows = grad_extended[:, 3:] + edge_pad
    grad_projected = jnp.concatenate([grad_conv_rows, grad_gate_rows[None]], axis=0).astype(
        jnp.bfloat16
    )
    grad_mix = jnp.einsum(
        "td,jtc->jdc", normed1_low, grad_projected, preferred_element_type=jnp.float32
    )
    grad_normed1 = head_total(
        jnp.einsum("jtc,jdc->td", grad_projected, mix_again, preferred_element_type=jnp.float32)
    )
    grad_rows1, grad_norm1 = token_norm_back(token_rows, inverse1, norm1_gain, grad_normed1)
    grad_tokens = grad_hidden + grad_rows1
    mix_part, up_part, out_part, down_part = (
        lax.psum_scatter(grad_mix, "seq", scatter_dimension=1, tiled=True),
        lax.psum_scatter(grad_up, "seq", scatter_dimension=1, tiled=True),
        lax.psum_scatter(grad_out, "seq", scatter_dimension=1, tiled=True),
        lax.psum_scatter(grad_down, "seq", scatter_dimension=1, tiled=True),
    )
    conv_total, gap_total, group_total, norm1_total, norm2_total = lax.psum(
        (grad_conv, grad_gap, grad_group, grad_norm1, grad_norm2), "seq"
    )
    inverse_rms = jnp.stack([inverse1[:, 0], inverse2[:, 0]])
    return (
        block_out,
        grad_tokens,
        norm1_total,
        mix_part,
        conv_total,
        gap_total,
        group_total,
        out_part,
        norm2_total,
        up_part,
        down_part,
        inverse_rms,
    )


def solution(mesh):
    in_specs = (
        P("seq", None),
        P(),
        P(None, "seq", "head"),
        P(None, None, "head"),
        P("head"),
        P("head"),
        P("head", "seq"),
        P(),
        P(None, "seq", "head"),
        P("head", "seq"),
        P("seq", None),
    )
    out_specs = (
        P("seq", None),
        P("seq", None),
        P(),
        P(None, "seq", "head"),
        P(None, None, "head"),
        P("head"),
        P("head"),
        P("head", "seq"),
        P(),
        P(None, "seq", "head"),
        P("head", "seq"),
        P(None, "seq"),
    )
    return jax.shard_map(shards, mesh=mesh, in_specs=in_specs, out_specs=out_specs, check_vma=False)
```

profile of v0, /device:TPU:10, one launch (start us, length us, event | category | flops | bytes accessed | tf_op | source)
XLA Modules:
  0.0 3646.1 jit_solution(11405974941305117379)
XLA Ops:
  9.8 191.8 %all-gather.13.cloned.1.call-done = bf16[4,2048,1024]{2,1,0:T(8,128)(2,1)} async-done(((bf16[4,128,1024]{2,1,0:T(8,128)(2,1)}), bf16[4,2048,1024]{2,1,0:T(8,128)(2,1)}) %all-gather.13.cloned.1.call-update) | async-done | bytes 16777232 | tf_op jit(solution)/shard_map/all_gather | solution.py:154
  218.7 12.9 fusion.119
  235.8 31.4 all_gather.47
  270.4 77.4 %all-gather.29.cloned.1.call-done = f32[128,128,128]{2,1,0:T(8,128)} async-done(((f32[8,128,128]{2,1,0:T(8,128)}), f32[128,128,128]{2,1,0:T(8,128)}) %all-gather.29.cloned.1.call-update) | async-done | bytes 8388624 | tf_op jit(solution)/shard_map/all_gather | solution.py:21
  347.8 22.9 while.70
  386.4 50.0 %all-gather.15.cloned.1.call-done = bf16[1024,2048]{1,0:T(8,128)(2,1)} async-done(((bf16[1024,128]{1,0:T(8,128)(2,1)}), bf16[1024,2048]{1,0:T(8,128)(2,1)}) %all-gather.15.cloned.1.call-update) | async-done | bytes 4194320 | tf_op jit(solution)/shard_map/all_gather | solution.py:156
  464.2 250.8 %all-gather.19.cloned.1.call-done = bf16[2,2048,2816]{2,1,0:T(8,128)(2,1)} async-done(((bf16[2,128,2816]{2,1,0:T(8,128)(2,1)}), bf16[2,2048,2816]{2,1,0:T(8,128)(2,1)}) %all-gather.19.cloned.1.call-update) | async-done | bytes 23068688 | tf_op jit(solution)/shard_map/all_gather | solution.py:155
  715.0 12.4 convolution_bitcast_fusion.6
  727.4 170.8 %all-gather.21.cloned.1.call-done = bf16[2816,2048]{1,0:T(8,128)(2,1)} async-done(((bf16[2816,128]{1,0:T(8,128)(2,1)}), bf16[2816,2048]{1,0:T(8,128)(2,1)}) %all-gather.21.cloned.1.call-update) | async-done | bytes 11534352 | tf_op jit(solution)/shard_map/all_gather | solution.py:157
  898.3 10.1 fusion.59
  909.5 12.9 convolution_bitcast_fusion.8
  932.4 12.5 reduce-scatter.11.cloned.1.call-done
  945.0 11.6 all-gather.25.cloned.1.call-done
  988.3 109.4 %all-gather.31.cloned.1.call-done = f32[128,128,128]{2,1,0:T(8,128)} async-done(((f32[8,128,128]{2,1,0:T(8,128)}), f32[128,128,128]{2,1,0:T(8,128)}) %all-gather.31.cloned.1.call-update) | async-done | bytes 8388624 | tf_op jit(solution)/shard_map/all_gather | solution.py:21
  1097.6 33.4 while.71
  1134.4 37.0 %while.68 = (s32[]{:T(128)}, f32[8,128,128]{2,1,0:T(8,128)S(1)}, f32[2,64,8,128]{3,2,1,0:T(8,128)}, f32[2,64,8,128]{3,2,1,0:T(8,128)}, f32[2,64,8,128]{3,2,1,0:T...) while((s32[]{:T(128)}, f32[8,128,128]{2,1,0:T(8,128)S(1)}, ...), condition=%wide.region_22.23_spmd, body=%wide.region_17.22_spmd.sunk | while | flops 665260032 | bytes 41624012 | solution.py:100
  1187.2 12.4 convolution_bitcast_fusion.7
  1222.9 13.4 convolution_bitcast_fusion.5
  1237.7 19.0 convolution_bitcast_fusion.4
  1275.8 58.3 %all-reduce.16.cloned.1.call-done = (f32[2048]{0:T(1024)}, f32[3,4,1024]{2,0,1:T(4,128)}, f32[1024]{0:T(1024)}, f32[1024]{0:T(1024)}, f32[2048]{0:T(1024)}) async-done(((f32[2048]{0:T(1024)}, f32[3,4,1024]{2,0,1:T(4,128)}, f32[1024]{0:T(1024)}, f32[1024]{0:T(1024)}, f32[2048]{0:T(1024)}), (f32[2048]{0:T(1024)}, f32[3,4,1024]{2,0,1:T(4,128)}, f32[1024]{0:T(1024)}, f32[1024]{0:T(1024)}, ...) | async-done | bytes 73744 | tf_op jit(solution)/shard_map/psum | solution.py:260
  1335.6 690.0 %reduce-scatter.17.cloned.1.call-done = f32[4,128,1024]{1,2,0:T(8,128)} async-done(((f32[4,2048,1024]{1,2,0:T(8,128)}), f32[4,128,1024]{1,2,0:T(8,128)}) %reduce-scatter.17.cloned.1.call-update) | async-done | bytes 2097168 | tf_op jit(solution)/shard_map/reduce_scatter | solution.py:255
  2028.4 942.6 %reduce-scatter.21.cloned.1.call-done = f32[2,128,2816]{1,2,0:T(8,128)} async-done(((f32[2,2048,2816]{1,2,0:T(8,128)}), f32[2,128,2816]{1,2,0:T(8,128)}) %reduce-scatter.21.cloned.1.call-update) | async-done | bytes 2883600 | tf_op jit(solution)/shard_map/reduce_scatter | solution.py:256
  2974.4 180.3 %reduce-scatter.19.cloned.1.call-done = f32[1024,128]{1,0:T(8,128)} async-done(((f32[1024,2048]{1,0:T(8,128)}), f32[1024,128]{1,0:T(8,128)}) %reduce-scatter.19.cloned.1.call-update) | async-done | bytes 524304 | tf_op jit(solution)/shard_map/reduce_scatter | solution.py:257
  3154.7 482.1 %reduce-scatter.23.cloned.1.call-done = f32[2816,128]{1,0:T(8,128)} async-done(((f32[2816,2048]{1,0:T(8,128)}), f32[2816,128]{1,0:T(8,128)}) %reduce-scatter.23.cloned.1.call-update) | async-done | bytes 1441808 | tf_op jit(solution)/shard_map/reduce_scatter | solution.py:258
  (449 shorter events, 285.5 us)
Async XLA Ops:
  7.2 194.4 %all-gather.13.cloned.1.call-start = ((), (), s32[]{:S(2)}) async-start(), calls=%async_computation.8 | async-start | bytes 17825792 | tf_op jit(solution)/shard_map/all_gather | solution.py:154
  7.9 339.9 %all-gather.29.cloned.1.call-start = ((), (), s32[]{:S(2)}) async-start(), calls=%async_computation.24 | async-start | bytes 8912896 | tf_op jit(solution)/shard_map/all_gather | solution.py:21
  209.8 5.7 collective-permute-start
  235.0 201.5 %all-gather.15.cloned.1.call-start = ((), (), s32[]{:S(2)}) async-start(), calls=%async_computation.9 | async-start | bytes 4456448 | tf_op jit(solution)/shard_map/all_gather | solution.py:156
  235.7 214.6 %reduce-scatter.9.cloned.1.call-start = ((), (), s32[]{:S(2)}) async-start(), calls=%async_computation.10 | async-start | bytes 1572864 | tf_op jit(solution)/shard_map/reduce_scatter | solution.py:136
  440.4 21.7 all-gather.17.cloned.1.call-start
  450.3 264.7 %all-gather.19.cloned.1.call-start = ((), (), s32[]{:S(2)}) async-start(), calls=%async_computation.12 | async-start | bytes 24510464 | tf_op jit(solution)/shard_map/all_gather | solution.py:155
  450.9 447.4 %all-gather.21.cloned.1.call-start = ((), (), s32[]{:S(2)}) async-start(), calls=%async_computation.13 | async-start | bytes 12255232 | tf_op jit(solution)/shard_map/all_gather | solution.py:157
  451.7 480.7 %reduce-scatter.13.cloned.1.call-start = ((), (), s32[]{:S(2)}) async-start(), calls=%async_computation.16 | async-start | bytes 1572864 | tf_op jit(solution)/shard_map/reduce_scatter | solution.py:136
  922.4 22.5 reduce-scatter.11.cloned.1.call-start
  929.6 27.0 all-gather.25.cloned.1.call-start
  932.4 36.1 all-gather.23.cloned.1.call-start
  944.9 152.7 %all-gather.31.cloned.1.call-start = ((), (), s32[]{:S(2)}) async-start(), calls=%async_computation.25 | async-start | bytes 8912896 | tf_op jit(solution)/shard_map/all_gather | solution.py:21
  985.1 223.9 %reduce-scatter.15.cloned.1.call-start = ((), (), s32[]{:S(2)}) async-start(), calls=%async_computation.18 | async-start | bytes 1572864 | tf_op jit(solution)/shard_map/reduce_scatter | solution.py:136
  1180.2 6.8 collective-permute-start.1
  1199.6 21.0 all-gather.27.cloned.1.call-start
  1209.1 125.0 %all-reduce.16.cloned.1.call-start = ((), (), s32[]{:S(2)}) async-start(), calls=%async_computation.26 | async-start | bytes 180224 | tf_op jit(solution)/shard_map/psum | solution.py:260
  1222.8 802.7 %reduce-scatter.17.cloned.1.call-start = ((), (), s32[]{:S(2)}) async-start(), calls=%async_computation.20 | async-start | bytes 35651584 | tf_op jit(solution)/shard_map/reduce_scatter | solution.py:255
  1236.3 1734.7 %reduce-scatter.21.cloned.1.call-start = ((), (), s32[]{:S(2)}) async-start(), calls=%async_computation.22 | async-start | bytes 49020928 | tf_op jit(solution)/shard_map/reduce_scatter | solution.py:256
  1256.7 1898.0 %reduce-scatter.19.cloned.1.call-start = ((), (), s32[]{:S(2)}) async-start(), calls=%async_computation.21 | async-start | bytes 8912896 | tf_op jit(solution)/shard_map/reduce_scatter | solution.py:257
  1262.5 2374.2 %reduce-scatter.23.cloned.1.call-start = ((), (), s32[]{:S(2)}) async-start(), calls=%async_computation.23 | async-start | bytes 24510464 | tf_op jit(solution)/shard_map/reduce_scatter | solution.py:258
  2028.4 1608.9 %copy-start.73 = (f32[1024]{0:T(1024)S(1)}, f32[1024]{0:T(1024)}, u32[]{:S(2)}) copy-start(f32[1024]{0:T(1024)} %get-tuple-element.1199) | copy-start | bytes 12292
  2028.4 1609.5 %copy-start.72 = (f32[1024]{0:T(1024)S(1)}, f32[1024]{0:T(1024)}, u32[]{:S(2)}) copy-start(f32[1024]{0:T(1024)} %get-tuple-element.1200) | copy-start | bytes 12292
  2028.4 1610.1 %copy-start.66 = (f32[2048]{0:T(1024)S(1)}, f32[2048]{0:T(1024)}, u32[]{:S(2)}) copy-start(f32[2048]{0:T(1024)} %get-tuple-element.1202) | copy-start | bytes 24580
  (87 other events, 3335.2 us)
Sparse Core Ops, SparseCore 0:
  10.8 190.7 all-gather.12
  235.1 112.6 all-gather.28
  350.5 85.8 all-gather.14
  440.5 9.7 reduce-scatter.8
  451.8 10.2 all-gather.16
  465.0 249.9 all-gather.18
  718.1 180.1 all-gather.20
  922.5 9.8 reduce-scatter.12
  935.2 9.6 reduce-scatter.10
  946.4 10.1 all-gather.24
  958.2 10.1 all-gather.22
  985.2 112.3 all-gather.30
  1199.7 9.2 reduce-scatter.14
  1210.4 10.1 all-gather.26
  1227.8 106.2 all-reduce.15
  1336.3 689.1 reduce-scatter.16
  2027.7 943.2 reduce-scatter.20
  2973.7 180.8 reduce-scatter.18
  3157.6 479.1 reduce-scatter.22
where the time goes:
time: 3660 us; the launch traced here: 3650 us
  waiting for transfers between devices  3290 us (90%)
  matrix products  140 us (4%)
  other arithmetic  105 us (3%)
  local copies, waits for them, and re-layouts  56.5 us (2%)
    reduce_scatter x1, waiting for transfers between devices, shards(): lax.psum_scatter(grad_up, 'seq', scatter_dimension=1, tiled=True)  943 us
    reduce_scatter x1, waiting for transfers between devices, shards(): lax.psum_scatter(grad_mix, 'seq', scatter_dimension=1, tiled=True)  690 us
    reduce_scatter x1, waiting for transfers between devices, shards(): lax.psum_scatter(grad_down, 'seq', scatter_dimension=1, tiled=True)  482 us
    all_gather x1, waiting for transfers between devices, shards(): lax.all_gather(up_pair, 'seq', axis=1, tiled=True)  251 us
    all_gather x1, waiting for transfers between devices, shards(): lax.all_gather(mix_weight, 'seq', axis=1, tiled=True)  192 us
    all_gather x2, waiting for transfers between devices, carried_in(): everything = jax.tree.map(lambda part: lax.all_gather(part, axis), array)  187 us
    reduce_scatter x1, waiting for transfers between devices, shards(): lax.psum_scatter(grad_out, 'seq', scatter_dimension=1, tiled=True)  180 us
    all_gather x1, waiting for transfers between devices, shards(): lax.all_gather(down_weight, 'seq', axis=1, tiled=True)  171 us
  transfers between devices with their start and end apart: 21, of which 21 were waited for; matrix products, arithmetic and copies ran while one was open for 3% of the time, Pallas kernels for 0%

commit v1 on v0

--- a/solution.py
+++ b/solution.py
@@ -8,6 +8,14 @@
 EPS_TOKEN = 1e-06
 EPS_GROUP = 1e-05
 HIGH = lax.Precision.HIGHEST
+
+
+def list_the_space(state, array_dim):
+    state = jnp.moveaxis(state, 0, array_dim)
+    x_new = state.shape
+    return state.reshape(
+        *x_new[:array_dim], x_new[array_dim] * x_new[array_dim + 1], *x_new[array_dim + 2 :]
+    )
 
 
 def from_behind(value, axis, steps):
@@ -150,9 +158,33 @@
     down_weight,
     cotangent,
 ):
+
+    def put_view(w_in, mesh_ax, pos_dim=1):
+        line_up = []
+        devs = lax.psum(1, mesh_ax)
+        for j in range(devs):
+            line_up.append((j, (j + 1) % devs))
+        made = []
+        for idx, pp in line_up:
+            made.append((pp, idx))
+        long_array, top = ([], [])
+        for jj in range(devs - 1):
+            if jj % 2 == 0:
+                outcome_arr = lax.ppermute(long_array[-1] if long_array else w_in, mesh_ax, line_up)
+                long_array.append(outcome_arr)
+            else:
+                q_next = lax.ppermute(top[-1] if top else w_in, mesh_ax, made)
+                top.append(q_next)
+        front = jnp.stack([*long_array[::-1], w_in, *top])
+        extra = len(long_array)
+        parts_out = lax.axis_index(mesh_ax)
+        z2 = parts_out - extra
+        front = front[(jnp.arange(devs) - z2) % devs]
+        return list_the_space(front, pos_dim)
+
     mix_full, up_full, out_full, down_full = (
         lax.all_gather(mix_weight, "seq", axis=1, tiled=True),
-        lax.all_gather(up_pair, "seq", axis=1, tiled=True),
+        put_view(up_pair, "seq"),
         lax.all_gather(out_weight, "seq", axis=1, tiled=True),
         lax.all_gather(down_weight, "seq", axis=1, tiled=True),
     )

time: 3660 us -> 3920 us (1.071)
  waiting for transfers between devices: 3290 us -> 3440 us
  local copies, waits for them, and re-layouts: 56.5 us -> 132 us
  starting transfers between devices: 7.93 us -> 52 us
    ppermute x0 -> x15, waiting for transfers between devices: none -> 530 us  [the longest x8 406 us: put_view(): lax.ppermute(long_array[-1] if long_array else w_in, mesh_ax, line_up)]
    all_gather x1, waiting for transfers between devices: 251 us -> 62 us  [shards(): lax.all_gather(up_pair, 'seq', axis=1, tiled=True)]
    all_gather x1, waiting for transfers between devices: 171 us -> 0.01 us  [shards(): lax.all_gather(down_weight, 'seq', axis=1, tiled=True)]
  transfers between devices with their start and end apart: 21 -> 36, of which waited for: 21 -> 32; matrix products, arithmetic and copies ran while one was open for 3% -> 5% of each run, Pallas kernels for 0% -> 0%
where the time goes in v1:
time: 3920 us; the launch traced here: 3910 us
  waiting for transfers between devices  3440 us (88%)
  matrix products  141 us (4%)
  local copies, waits for them, and re-layouts  132 us (3%)
  other arithmetic  98.5 us (3%)
  starting transfers between devices  52 us (1%)
    reduce_scatter x1, waiting for transfers between devices, shards(): lax.psum_scatter(grad_up, 'seq', scatter_dimension=1, tiled=True)  943 us
    reduce_scatter x1, waiting for transfers between devices, shards(): lax.psum_scatter(grad_mix, 'seq', scatter_dimension=1, tiled=True)  690 us
    reduce_scatter x1, waiting for transfers between devices, shards(): lax.psum_scatter(grad_down, 'seq', scatter_dimension=1, tiled=True)  482 us
    ppermute x8, waiting for transfers between devices, put_view(): lax.ppermute(long_array[-1] if long_array else w_in, mesh_ax, line_up)  406 us
    all_gather x1, waiting for transfers between devices, shards(): lax.all_gather(mix_weight, 'seq', axis=1, tiled=True)  191 us
    all_gather x2, waiting for transfers between devices, carried_in(): everything = jax.tree.map(lambda part: lax.all_gather(part, axis), array)  188 us
    reduce_scatter x1, waiting for transfers between devices, shards(): lax.psum_scatter(grad_out, 'seq', scatter_dimension=1, tiled=True)  180 us
    ppermute x7, waiting for transfers between devices, put_view(): q_next = lax.ppermute(top[-1] if top else w_in, mesh_ax, made)  124 us
  transfers between devices with their start and end apart: 36, of which 32 were waited for; matrix products, arithmetic and copies ran while one was open for 5% of the time, Pallas kernels for 0%

profile of v1, /device:TPU:10, one launch (start us, length us, event | category | flops | bytes accessed | tf_op | source)
XLA Modules:
  0.0 3909.5 jit_solution(3483347788495604902)
XLA Ops:
  10.8 190.7 %all-gather.13.cloned.1.call-done = bf16[4,2048,1024]{2,1,0:T(8,128)(2,1)} async-done(((bf16[4,128,1024]{2,1,0:T(8,128)(2,1)}), bf16[4,2048,1024]{2,1,0:T(8,128)(2,1)}) %all-gather.13.cloned.1.call-update) | async-done | bytes 16777232 | tf_op jit(solution)/shard_map/all_gather | solution.py:186
  224.0 31.4 all_gather.46
  257.5 78.5 %all-gather.29.cloned.1.call-done = f32[128,128,128]{2,1,0:T(8,128)} async-done(((f32[8,128,128]{2,1,0:T(8,128)}), f32[128,128,128]{2,1,0:T(8,128)}) %all-gather.29.cloned.1.call-update) | async-done | bytes 8388624 | tf_op jit(solution)/shard_map/all_gather | solution.py:29
  336.0 22.9 while.70
  379.6 45.1 %all-gather.15.cloned.1.call-done = bf16[1024,2048]{1,0:T(8,128)(2,1)} async-done(((bf16[1024,128]{1,0:T(8,128)(2,1)}), bf16[1024,2048]{1,0:T(8,128)(2,1)}) %all-gather.15.cloned.1.call-update) | async-done | bytes 4194320 | tf_op jit(solution)/shard_map/all_gather | solution.py:188
  441.4 40.3 %collective-permute-done.1 = bf16[2,128,2816]{2,1,0:T(8,128)(2,1)S(1)} collective-permute-done((bf16[2,128,2816]{2,1,0:T(8,128)(2,1)}, bf16[2,128,2816]{2,1,0:T(8,128)(2,1)S(1)}, u32[]{:S(2)}, u32[]{:S(2)}) %collective-permute-start.1) | collective-permute-done | bytes 1441824 | tf_op jit(solution)/shard_map/ppermute | solution.py:173
  485.5 59.0 %collective-permute-done.2 = bf16[2,128,2816]{2,1,0:T(8,128)(2,1)S(1)} collective-permute-done((bf16[2,128,2816]{2,1,0:T(8,128)(2,1)S(1)}, bf16[2,128,2816]{2,1,0:T(8,128)(2,1)S(1)}, u32[]{:S(2)}, u32[]{:S(2)}) %collective-permute-start.2) | collective-permute-done | bytes 1441824 | tf_op jit(solution)/shard_map/ppermute | solution.py:173
  551.8 69.1 %collective-permute-done.3 = bf16[2,128,2816]{2,1,0:T(8,128)(2,1)S(1)} collective-permute-done((bf16[2,128,2816]{2,1,0:T(8,128)(2,1)S(1)}, bf16[2,128,2816]{2,1,0:T(8,128)(2,1)S(1)}, u32[]{:S(2)}, u32[]{:S(2)}) %collective-permute-start.3) | collective-permute-done | bytes 1441824 | tf_op jit(solution)/shard_map/ppermute | solution.py:173
  623.6 91.6 %collective-permute-done.4 = bf16[2,128,2816]{2,1,0:T(8,128)(2,1)S(1)} collective-permute-done((bf16[2,128,2816]{2,1,0:T(8,128)(2,1)S(1)}, bf16[2,128,2816]{2,1,0:T(8,128)(2,1)S(1)}, u32[]{:S(2)}, u32[]{:S(2)}) %collective-permute-start.4) | collective-permute-done | bytes 1441824 | tf_op jit(solution)/shard_map/ppermute | solution.py:173
  736.3 57.6 %collective-permute-done.5 = bf16[2,128,2816]{2,1,0:T(8,128)(2,1)S(1)} collective-permute-done((bf16[2,128,2816]{2,1,0:T(8,128)(2,1)S(1)}, bf16[2,128,2816]{2,1,0:T(8,128)(2,1)S(1)}, u32[]{:S(2)}, u32[]{:S(2)}) %collective-permute-start.5) | collective-permute-done | bytes 1441824 | tf_op jit(solution)/shard_map/ppermute | solution.py:173
  799.2 27.3 collective-permute-done.6
  838.4 37.6 collective-permute-done.13
  878.4 30.7 collective-permute-done.7
  916.5 59.5 %collective-permute-done.14 = bf16[2,128,2816]{2,1,0:T(8,128)(2,1)} collective-permute-done((bf16[2,128,2816]{2,1,0:T(8,128)(2,1)}, bf16[2,128,2816]{2,1,0:T(8,128)(2,1)}, u32[]{:S(2)}, u32[]{:S(2)}) %collective-permute-start.14) | collective-permute-done | bytes 1441824 | tf_op jit(solution)/shard_map/ppermute | solution.py:176
  976.0 30.1 collective-permute-done.8
  1102.5 62.0 %all-gather.23.cloned.1.call-done = bf16[2,2048,2816]{2,1,0:T(8,128)(2,1)} async-done(((bf16[2,128,2816]{2,1,0:T(8,128)(2,1)}), bf16[2,2048,2816]{2,1,0:T(8,128)(2,1)}) %all-gather.23.cloned.1.call-update) | async-done | bytes 23068688 | tf_op jit(solution)/shard_map/all_gather | solution.py:235
  1249.1 109.5 %all-gather.31.cloned.1.call-done = f32[128,128,128]{2,1,0:T(8,128)} async-done(((f32[8,128,128]{2,1,0:T(8,128)}), f32[128,128,128]{2,1,0:T(8,128)}) %all-gather.31.cloned.1.call-update) | async-done | bytes 8388624 | tf_op jit(solution)/shard_map/all_gather | solution.py:29
  1358.7 33.4 while.71
  1395.4 39.4 %while.68 = (s32[]{:T(128)}, f32[8,128,128]{2,1,0:T(8,128)S(1)}, f32[2,64,8,128]{3,2,1,0:T(8,128)}, f32[2,64,8,128]{3,2,1,0:T(8,128)}, f32[2,64,8,128]{3,2,1,0:T...) while((s32[]{:T(128)}, f32[8,128,128]{2,1,0:T(8,128)S(1)}, ...), condition=%wide.region_22.23_spmd, body=%wide.region_17.22_spmd.sunk | while | flops 665260032 | bytes 37429652 | solution.py:108
  1539.2 58.3 %all-reduce.16.cloned.1.call-done = (f32[2048]{0:T(1024)}, f32[3,4,1024]{2,0,1:T(4,128)}, f32[1024]{0:T(1024)}, f32[1024]{0:T(1024)}, f32[2048]{0:T(1024)}) async-done(((f32[2048]{0:T(1024)}, f32[3,4,1024]{2,0,1:T(4,128)}, f32[1024]{0:T(1024)}, f32[1024]{0:T(1024)}, f32[2048]{0:T(1024)}), (f32[2048]{0:T(1024)}, f32[3,4,1024]{2,0,1:T(4,128)}, f32[1024]{0:T(1024)}, f32[1024]{0:T(1024)}, ...) | async-done | bytes 73744 | tf_op jit(solution)/shard_map/psum | solution.py:292
  1599.0 690.0 %reduce-scatter.17.cloned.1.call-done = f32[4,128,1024]{1,2,0:T(8,128)} async-done(((f32[4,2048,1024]{1,2,0:T(8,128)}), f32[4,128,1024]{1,2,0:T(8,128)}) %reduce-scatter.17.cloned.1.call-update) | async-done | bytes 2097168 | tf_op jit(solution)/shard_map/reduce_scatter | solution.py:287
  2291.8 942.6 %reduce-scatter.21.cloned.1.call-done = f32[2,128,2816]{1,2,0:T(8,128)} async-done(((f32[2,2048,2816]{1,2,0:T(8,128)}), f32[2,128,2816]{1,2,0:T(8,128)}) %reduce-scatter.21.cloned.1.call-update) | async-done | bytes 2883600 | tf_op jit(solution)/shard_map/reduce_scatter | solution.py:288
  3237.8 180.3 %reduce-scatter.19.cloned.1.call-done = f32[1024,128]{1,0:T(8,128)} async-done(((f32[1024,2048]{1,0:T(8,128)}), f32[1024,128]{1,0:T(8,128)}) %reduce-scatter.19.cloned.1.call-update) | async-done | bytes 524304 | tf_op jit(solution)/shard_map/reduce_scatter | solution.py:289
  3418.0 482.1 %reduce-scatter.23.cloned.1.call-done = f32[2816,128]{1,0:T(8,128)} async-done(((f32[2816,2048]{1,0:T(8,128)}), f32[2816,128]{1,0:T(8,128)}) %reduce-scatter.23.cloned.1.call-update) | async-done | bytes 1441808 | tf_op jit(solution)/shard_map/reduce_scatter | solution.py:290
  (507 shorter events, 532.3 us)
Async XLA Ops:
  7.2 194.4 %all-gather.13.cloned.1.call-start = ((), (), s32[]{:S(2)}) async-start(), calls=%async_computation.8 | async-start | bytes 17825792 | tf_op jit(solution)/shard_map/all_gather | solution.py:186
  7.9 328.1 %all-gather.29.cloned.1.call-start = ((), (), s32[]{:S(2)}) async-start(), calls=%async_computation.24 | async-start | bytes 8912896 | tf_op jit(solution)/shard_map/all_gather | solution.py:29
  223.2 201.5 %all-gather.15.cloned.1.call-start = ((), (), s32[]{:S(2)}) async-start(), calls=%async_computation.9 | async-start | bytes 4456448 | tf_op jit(solution)/shard_map/all_gather | solution.py:188
  223.9 214.6 %reduce-scatter.9.cloned.1.call-start = ((), (), s32[]{:S(2)}) async-start(), calls=%async_computation.10 | async-start | bytes 1572864 | tf_op jit(solution)/shard_map/reduce_scatter | solution.py:144
  428.6 648.7 %all-gather.17.cloned.1.call-start = ((), (), s32[]{:S(2)}) async-start(), calls=%async_computation.11 | async-start | bytes 1572864 | tf_op jit(solution)/shard_map/all_gather | solution.py:145
  438.6 653.8 %all-gather.19.cloned.1.call-start = ((), (), s32[]{:S(2)}) async-start(), calls=%async_computation.12 | async-start | bytes 12255232 | tf_op jit(solution)/shard_map/all_gather | solution.py:189
  439.1 725.4 %all-gather.23.cloned.1.call-start = ((), (), s32[]{:S(2)}) async-start(), calls=%async_computation.15 | async-start | bytes 24510464 | tf_op jit(solution)/shard_map/all_gather | solution.py:235
  439.9 757.3 %reduce-scatter.13.cloned.1.call-start = ((), (), s32[]{:S(2)}) async-start(), calls=%async_computation.16 | async-start | bytes 1572864 | tf_op jit(solution)/shard_map/reduce_scatter | solution.py:144
  544.5 76.4 %collective-permute-start.3 = (bf16[2,128,2816]{2,1,0:T(8,128)(2,1)S(1)}, bf16[2,128,2816]{2,1,0:T(8,128)(2,1)S(1)}, u32[]{:S(2)}, u32[]{:S(2)}) collective-permute-start(bf16[2,128,2816]{2,1,0:T(8,128)(2,1)S(1)} %collective-permute-done.2), channel_id=1, source_target_pairs={{0,2},{2,4},{4,6},{6,8},{8,10},{10,12},{12,14},{14,16},{16,18},{18... | collective-permute-start | bytes 4325384 | tf_op jit(solution)/shard_map/ppermute | solution.py:173
  550.3 71.1 %collective-permute-start.10 = (bf16[2,128,2816]{2,1,0:T(8,128)(2,1)S(1)}, bf16[2,128,2816]{2,1,0:T(8,128)(2,1)S(1)}, u32[]{:S(2)}, u32[]{:S(2)}) collective-permute-start(bf16[2,128,2816]{2,1,0:T(8,128)(2,1)S(1)} %collective-permute-done.9), channel_id=1, source_target_pairs={{2,0},{4,2},{6,4},{8,6},{10,8},{12,10},{14,12},{16,14},{18,16},{20... | collective-permute-start | bytes 4325384 | tf_op jit(solution)/shard_map/ppermute | solution.py:176
  620.9 94.4 %collective-permute-start.4 = (bf16[2,128,2816]{2,1,0:T(8,128)(2,1)S(1)}, bf16[2,128,2816]{2,1,0:T(8,128)(2,1)S(1)}, u32[]{:S(2)}, u32[]{:S(2)}) collective-permute-start(bf16[2,128,2816]{2,1,0:T(8,128)(2,1)S(1)} %collective-permute-done.3), channel_id=1, source_target_pairs={{0,2},{2,4},{4,6},{6,8},{8,10},{10,12},{12,14},{14,16},{16,18},{18... | collective-permute-start | bytes 4325384 | tf_op jit(solution)/shard_map/ppermute | solution.py:173
  621.4 113.3 %collective-permute-start.11 = (bf16[2,128,2816]{2,1,0:T(8,128)(2,1)S(1)}, bf16[2,128,2816]{2,1,0:T(8,128)(2,1)S(1)}, u32[]{:S(2)}, u32[]{:S(2)}) collective-permute-start(bf16[2,128,2816]{2,1,0:T(8,128)(2,1)S(1)} %collective-permute-done.10), channel_id=1, source_target_pairs={{2,0},{4,2},{6,4},{8,6},{10,8},{12,10},{14,12},{16,14},{18,16},{20... | collective-permute-start | bytes 4325384 | tf_op jit(solution)/shard_map/ppermute | solution.py:176
  715.2 78.7 %collective-permute-start.5 = (bf16[2,128,2816]{2,1,0:T(8,128)(2,1)S(1)}, bf16[2,128,2816]{2,1,0:T(8,128)(2,1)S(1)}, u32[]{:S(2)}, u32[]{:S(2)}) collective-permute-start(bf16[2,128,2816]{2,1,0:T(8,128)(2,1)S(1)} %collective-permute-done.4), channel_id=1, source_target_pairs={{0,2},{2,4},{4,6},{6,8},{8,10},{10,12},{12,14},{14,16},{16,18},{18... | collective-permute-start | bytes 4325384 | tf_op jit(solution)/shard_map/ppermute | solution.py:173
  797.6 78.4 %collective-permute-start.13 = (bf16[2,128,2816]{2,1,0:T(8,128)(2,1)S(1)}, bf16[2,128,2816]{2,1,0:T(8,128)(2,1)}, u32[]{:S(2)}, u32[]{:S(2)}) collective-permute-start(bf16[2,128,2816]{2,1,0:T(8,128)(2,1)S(1)} %collective-permute-done.12), channel_id=1, source_target_pairs={{2,0},{4,2},{6,4},{8,6},{10,8},{12,10},{14,12},{16,14},{18,16},{20... | collective-permute-start | bytes 4325384 | tf_op jit(solution)/shard_map/ppermute | solution.py:176
  826.5 82.6 %collective-permute-start.7 = (bf16[2,128,2816]{2,1,0:T(8,128)(2,1)S(1)}, bf16[2,128,2816]{2,1,0:T(8,128)(2,1)}, u32[]{:S(2)}, u32[]{:S(2)}) collective-permute-start(bf16[2,128,2816]{2,1,0:T(8,128)(2,1)S(1)} %collective-permute-done.6), channel_id=1, source_target_pairs={{0,2},{2,4},{4,6},{6,8},{8,10},{10,12},{12,14},{14,16},{16,18},{18... | collective-permute-start | bytes 4325384 | tf_op jit(solution)/shard_map/ppermute | solution.py:173
  876.0 100.0 %collective-permute-start.14 = (bf16[2,128,2816]{2,1,0:T(8,128)(2,1)}, bf16[2,128,2816]{2,1,0:T(8,128)(2,1)}, u32[]{:S(2)}, u32[]{:S(2)}) collective-permute-start(bf16[2,128,2816]{2,1,0:T(8,128)(2,1)} %collective-permute-done.13), channel_id=1, source_target_pairs={{2,0},{4,2},{6,4},{8,6},{10,8},{12,10},{14,12},{16,14},{18,16},{20... | collective-permute-start | bytes 4325384 | tf_op jit(solution)/shard_map/ppermute | solution.py:176
  909.1 97.0 %collective-permute-start.8 = (bf16[2,128,2816]{2,1,0:T(8,128)(2,1)}, bf16[2,128,2816]{2,1,0:T(8,128)(2,1)}, u32[]{:S(2)}, u32[]{:S(2)}) collective-permute-start(bf16[2,128,2816]{2,1,0:T(8,128)(2,1)} %collective-permute-done.7), channel_id=1, source_target_pairs={{0,2},{2,4},{4,6},{6,8},{8,10},{10,12},{12,14},{14,16},{16,18},{18... | collective-permute-start | bytes 4325384 | tf_op jit(solution)/shard_map/ppermute | solution.py:173
  1206.5 152.1 %all-gather.31.cloned.1.call-start = ((), (), s32[]{:S(2)}) async-start(), calls=%async_computation.25 | async-start | bytes 8912896 | tf_op jit(solution)/shard_map/all_gather | solution.py:29
  1246.1 226.2 %reduce-scatter.15.cloned.1.call-start = ((), (), s32[]{:S(2)}) async-start(), calls=%async_computation.18 | async-start | bytes 1572864 | tf_op jit(solution)/shard_map/reduce_scatter | solution.py:144
  1472.4 125.1 %all-reduce.16.cloned.1.call-start = ((), (), s32[]{:S(2)}) async-start(), calls=%async_computation.26 | async-start | bytes 180224 | tf_op jit(solution)/shard_map/psum | solution.py:292
  1486.1 802.8 %reduce-scatter.17.cloned.1.call-start = ((), (), s32[]{:S(2)}) async-start(), calls=%async_computation.20 | async-start | bytes 35651584 | tf_op jit(solution)/shard_map/reduce_scatter | solution.py:287
  1499.6 1734.8 %reduce-scatter.21.cloned.1.call-start = ((), (), s32[]{:S(2)}) async-start(), calls=%async_computation.22 | async-start | bytes 49020928 | tf_op jit(solution)/shard_map/reduce_scatter | solution.py:288
  1520.1 1897.9 %reduce-scatter.19.cloned.1.call-start = ((), (), s32[]{:S(2)}) async-start(), calls=%async_computation.21 | async-start | bytes 8912896 | tf_op jit(solution)/shard_map/reduce_scatter | solution.py:289
  1526.0 2374.2 %reduce-scatter.23.cloned.1.call-start = ((), (), s32[]{:S(2)}) async-start(), calls=%async_computation.23 | async-start | bytes 24510464 | tf_op jit(solution)/shard_map/reduce_scatter | solution.py:290
  (106 other events, 8515.1 us)
Sparse Core Ops, SparseCore 0:
  10.8 190.7 all-gather.12
  223.3 112.6 all-gather.28
  338.7 85.8 all-gather.14
  428.7 9.8 reduce-scatter.8
  440.0 10.1 all-gather.16
  453.2 336.8 all-gather.18
  793.2 371.2 all-gather.22
  1177.9 9.1 reduce-scatter.12
  1197.3 9.1 reduce-scatter.10
  1208.0 10.1 all-gather.24
  1219.8 10.1 all-gather.20
  1246.3 112.3 all-gather.30
  1463.1 9.2 reduce-scatter.14
  1473.7 10.1 all-gather.26
  1491.1 106.2 all-reduce.15
  1599.7 689.1 reduce-scatter.16
  2291.1 943.2 reduce-scatter.20
  3237.1 180.8 reduce-scatter.18
  3420.9 479.1 reduce-scatter.22
